TPU v7x, 256 devices: a whole 4x4x8 slice. The times are simulated.
256 devices in a mesh: seq: 128 (over y_lo, z, x, core), dp: 2 (over y_hi).
Axes of the slice: x: 4, y: 4 (y_hi: 2, y_lo: 2; y = y_hi * 2 + y_lo), z: 8, core: 2. Of those that a mesh axis runs over, the one named last changes fastest.
Arguments:
- activations: bfloat16 [2, 512, 512, 768], P('dp', 'seq'), may hold values from -6 to 6
- grad_output: bfloat16 [2, 512, 512, 768], P('dp', 'seq'), may hold values from -24 to 24
- outer_factor: bfloat16 [512, 512], replicated, may hold values from -0.25 to 0.25
- inner_factor: bfloat16 [512, 512], replicated, may hold values from -0.25 to 0.25
- twiddle: float32 [512, 512], P('seq'), may hold values from 0.5 to 2
Outputs:
- grad_input: bfloat16 [2, 512, 512, 768], P('dp', 'seq')
- grad_outer: float32 [512, 512], P('seq')
- grad_inner: float32 [512, 512], P('seq')
- grad_twiddle: float32 [512, 512], P('seq')
All inputs are finite; a program needn't handle non-finite values.
Results may differ from a plain program's by a relative error of at most 0.0061.
Values may be sent and summed in bfloat16 or wider, within the bound.
A program may use at most 128 MiB of HBM per device.

v0:
```python
import jax
import jax.numpy as jnp
from jax import lax
from jax.sharding import PartitionSpec as P


def per_device(activations, grad_output, outer_factor, inner_factor, twiddle):
    acts = activations[0]
    grads_out = grad_output[0]
    inner = jnp.einsum("kj,ijc->ikc", inner_factor, acts, preferred_element_type=jnp.float32)
    scaled = (inner * twiddle[:, :, None]).astype(jnp.bfloat16)
    grads_f = grads_out.astype(jnp.float32)
    grad_mixed = (grads_f * acts.astype(jnp.float32)).astype(jnp.bfloat16)
    piece = lax.all_to_all(scaled, "seq", split_axis=1, concat_axis=0, tiled=True)
    mixed_piece = jnp.einsum("ab,bjc->ajc", outer_factor, piece, preferred_element_type=jnp.float32)
    mixed_cols = mixed_piece.astype(jnp.bfloat16)
    mixed_rows = lax.all_to_all(mixed_cols, "seq", split_axis=0, concat_axis=1, tiled=True)
    backward_piece = lax.all_to_all(grad_mixed, "seq", split_axis=1, concat_axis=0, tiled=True)
    grad_piece = jnp.einsum(
        "ab,ajc->bjc", outer_factor, backward_piece, preferred_element_type=jnp.float32
    )
    grad_scaled_cols = grad_piece.astype(jnp.bfloat16)
    grad_scaled = lax.all_to_all(grad_scaled_cols, "seq", split_axis=0, concat_axis=1, tiled=True)
    grad_gate = grads_f * mixed_rows.astype(jnp.float32)
    outer_term = jnp.einsum(
        "ajc,bjc->ab", backward_piece, piece, preferred_element_type=jnp.float32
    )
    grad_scaled_f = grad_scaled.astype(jnp.float32)
    twiddle_term = jnp.sum(grad_scaled_f * inner, axis=2)
    grad_inner_act = (grad_scaled_f * twiddle[:, :, None]).astype(jnp.bfloat16)
    inner_term = jnp.einsum("ikc,ijc->kj", grad_inner_act, acts, preferred_element_type=jnp.float32)
    back_inner = jnp.einsum(
        "kj,ikc->ijc", inner_factor, grad_inner_act, preferred_element_type=jnp.float32
    )
    grad_input = (grad_gate + back_inner).astype(jnp.bfloat16)[None]
    outer_total, inner_total = lax.psum((outer_term, inner_term), ("seq", "dp"))
    twiddle_total = lax.psum(twiddle_term, "dp")
    outer_rows = outer_total.shape[0] // lax.axis_size("seq")
    inner_rows = inner_total.shape[0] // lax.axis_size("seq")
    position = lax.axis_index("seq")
    grad_outer = lax.dynamic_slice_in_dim(outer_total, position * outer_rows, outer_rows, 0)
    grad_inner = lax.dynamic_slice_in_dim(inner_total, position * inner_rows, inner_rows, 0)
    return (grad_input, grad_outer, grad_inner, twiddle_total)


def solution(mesh):
    placed = (P("dp", "seq", None, None), P("dp", "seq", None, None), P(), P(), P("seq", None))
    return jax.shard_map(
        per_device,
        mesh=mesh,
        in_specs=placed,
        out_specs=(P("dp", "seq", None, None), P("seq", None), P("seq", None), P("seq", None)),
        check_vma=False,
    )
```

profile of v0, /device:TPU:1, one launch (start us, length us, event | category | flops | bytes accessed | tf_op | source)
XLA Modules:
  0.0 662.0 jit_solution(12997558020409800249)
XLA Ops:
  7.2 4.7 copy.40
  11.9 4.7 copy.41
  16.5 5.5 fusion.2
  22.0 6.1 copy.48
  28.1 90.7 %all_to_all.54 = bf16[4,512,768]{2,0,1:T(4,128)(2,1)S(1)} all-to-all(bf16[4,512,768]{2,0,1:T(4,128)(2,1)} %copy.48), channel_id=1, replica_groups=mesh['seq'=128,'dp'=2] {'seq'}, dimensions={1} | all-to-all | bytes 6291456 | tf_op jit(solution)/shard_map/all_to_all | solution.py:18
  118.8 1.2 copy.49
  120.1 1.6 copy-done.1
  121.7 3.5 convert_bitcast_fusion.2
  125.2 6.1 copy.51
  131.3 81.1 %all_to_all.55 = bf16[512,4,768]{2,1,0:T(4,128)(2,1)S(1)} all-to-all(bf16[512,4,768]{2,1,0:T(4,128)(2,1)} %copy.51), channel_id=1, replica_groups=mesh['seq'=128,'dp'=2] {'seq'}, dimensions={0} | all-to-all | bytes 6291456 | tf_op jit(solution)/shard_map/all_to_all | solution.py:23
  212.3 1.8 convert_bitcast_fusion
  214.1 4.3 copy.52
  218.4 7.6 %copy.53 = f32[4,512,768]{1,2,0:T(8,128)} copy(f32[4,512,768]{2,0,1:T(4,128)} %bitcast.67) | data formatting | bytes 12582912 | tf_op jit(solution)/shard_map/convert_element_type | solution.py:28
  226.0 7.4 %fusion.4 = (f32[4,512]{1,0:T(4,128)S(1)}, bf16[4,512,768]{1,2,0:T(8,128)(2,1)}) fusion(f32[4,512,768]{1,2,0:T(8,128)} %copy.53, f32[4,512]{1,0:T(4,128)S(1)} %copy-done.5, bf16[512,512]{1,0:T(8,128)(2,1)S(1)} %copy-done, bf16[1,4,512,768]{3,2,1,0:T(8,128)(2,1)} %param.5), kind=kOutput, calls=%fused_computation.10 | convolution fusion | flops 1616902144 | bytes 13123584 | tf_op jit(solution)/shard_map/kj,ijc->ikc/dot_general | solution.py:10
  233.4 6.2 copy.42
  239.6 81.1 %all_to_all.56 = bf16[4,512,768]{2,0,1:T(4,128)(2,1)S(1)} all-to-all(bf16[4,512,768]{2,0,1:T(4,128)(2,1)} %copy.42), channel_id=1, replica_groups=mesh['seq'=128,'dp'=2] {'seq'}, dimensions={1} | all-to-all | bytes 6291456 | tf_op jit(solution)/shard_map/all_to_all | solution.py:14
  320.6 1.2 copy.43
  321.9 1.7 copy-done.3
  323.5 3.5 convert_bitcast_fusion.3
  327.0 6.1 copy.45
  333.2 6.6 %all-to-all-start.1 = ((bf16[512,4,768]{2,1,0:T(4,128)(2,1)}), bf16[512,4,768]{2,1,0:T(4,128)(2,1)}, u32[]{:S(2)}, u32[]{:S(2)}) async-start(bf16[512,4,768]{2,1,0:T(4,128)(2,1)} %copy.45), calls=%async_computation.1 | async-start | bytes 6291456 | tf_op jit(solution)/shard_map/all_to_all | solution.py:17
  339.8 0.0 all-reduce.3.cloned.1.call-start
  339.9 6.7 %fusion.26 = f32[512,512]{1,0:T(8,128)} fusion(bf16[1,4,512,768]{3,2,1,0:T(8,128)(2,1)} %param.5, f32[4,512,768]{1,2,0:T(8,128)} %copy.53, f32[4,512]{1,0:T(4,128)S(1)} %copy-done.5), kind=kOutput, calls=%fused_computation.27 | convolution fusion | flops 1613758464 | bytes 10493952 | tf_op jit(solution)/shard_map/ikc,ijc->kj/dot_general | solution.py:31
  346.6 2.8 fusion.21
  349.5 6.5 psum.23
  355.9 268.6 %all-reduce.3.cloned.1.call-done = (f32[512,512]{1,0:T(8,128)}, f32[512,512]{1,0:T(8,128)}) async-done(((f32[512,512]{1,0:T(8,128)}, f32[512,512]{1,0:T(8,128)}), (f32[512,512]{1,0:T(8,128)}, f32[512,512]{1,0:T(8,128)})) %all-reduce.3.cloned.1.call-update) | async-done | bytes 2097168 | tf_op jit(solution)/shard_map/psum | solution.py:36
  624.5 1.3 constant_dynamic-slice_fusion
  625.9 3.7 convert_bitcast_fusion.1
  629.6 4.2 copy.46
  633.8 7.6 %copy.47 = f32[4,512,768]{1,2,0:T(8,128)} copy(f32[4,512,768]{2,0,1:T(4,128)} %bitcast.68) | data formatting | bytes 12582912 | tf_op jit(solution)/shard_map/convert_element_type | solution.py:24
  641.4 9.1 %fusion.5 = bf16[1,4,512,768]{2,3,1,0:T(8,128)(2,1)} fusion(f32[4,512,768]{1,2,0:T(8,128)} %copy.47, bf16[1,4,512,768]{2,3,1,0:T(8,128)(2,1)} %copy.40, f32[4,512,768]{1,2,0:T(8,128)} %copy.53, f32[4,512]{1,0:T(4,128)S(1)} %copy-done.5, bf16[512,512]{1,0:T(8,128)(2,1)S(1)} %copy-done), kind=kOutput, calls=%fused_computation.12 | convolution fusion | flops 1620049920 | bytes 19406848 | tf_op jit(solution)/shard_map/kj,ikc->ijc/dot_general | solution.py:32
  650.5 4.6 copy.59
  (14 shorter events, 0.0 us)
Async XLA Ops:
  7.2 218.8 %copy-start = (bf16[512,512]{1,0:T(8,128)(2,1)S(1)}, bf16[512,512]{1,0:T(8,128)(2,1)}, u32[]{:S(2)}) copy-start(bf16[512,512]{1,0:T(8,128)(2,1)} %param.8) | copy-start | bytes 1572868
  118.8 2.9 copy-start.6
  120.0 1.6 copy-start.1
  218.4 7.6 %copy-start.5 = (f32[4,512]{1,0:T(4,128)S(1)}, f32[4,512]{1,0:T(4,128)}, u32[]{:S(2)}) copy-start(f32[4,512]{1,0:T(4,128)} %param.9) | copy-start | bytes 24580
  321.9 1.7 copy-start.3
  333.2 292.7 %all-to-all-start.1 = ((bf16[512,4,768]{2,1,0:T(4,128)(2,1)}), bf16[512,4,768]{2,1,0:T(4,128)(2,1)}, u32[]{:S(2)}, u32[]{:S(2)}) async-start(bf16[512,4,768]{2,1,0:T(4,128)(2,1)} %copy.45), calls=%async_computation.1 | async-start | bytes 6291456 | tf_op jit(solution)/shard_map/all_to_all | solution.py:17
  339.8 284.7 %all-reduce.3.cloned.1.call-start = ((), (), s32[]{:S(2)}) async-start(), calls=%async_computation.4 | async-start | bytes 4194304 | tf_op jit(solution)/shard_map/psum | solution.py:36
  339.9 6.7 %copy-start.2 = (bf16[128,4,4,768]{3,2,1,0:T(4,128)(2,1)S(1)}, bf16[128,4,4,768]{3,2,1,0:T(4,128)(2,1)}, u32[]{:S(2)}) copy-start(bf16[128,4,4,768]{3,2,1,0:T(4,128)(2,1)} %copy-done.1) | copy-start | bytes 9437188
  339.9 6.7 %copy-start.4 = (bf16[128,4,4,768]{3,2,1,0:T(4,128)(2,1)S(1)}, bf16[128,4,4,768]{3,2,1,0:T(4,128)(2,1)}, u32[]{:S(2)}) copy-start(bf16[128,4,4,768]{3,2,1,0:T(4,128)(2,1)} %copy-done.3) | copy-start | bytes 9437188
Sparse Core Ops, SparseCore 0:
  349.6 274.8 all-reduce.2
where the time goes:
time: 664 us; the launch traced here: 662 us
  waiting for transfers between devices  269 us (41%)
  blocking collectives  259 us (39%)
  local copies, waits for them, and re-layouts  69.2 us (10%)
  matrix products  33.1 us (5%)
  between operations  14.1 us (2%)
  other arithmetic  11 us (2%)
  starting transfers between devices  6.69 us (1%)
    psum x1, waiting for transfers between devices, per_device(): outer_total, inner_total = lax.psum((outer_term, inner_term), ('seq', 'dp'))  269 us
    all_to_all x1, blocking collectives, per_device(): lax.all_to_all(grad_mixed, 'seq', split_axis=1, concat_axis=0, tiled=True)  90.7 us
    all_to_all x1, blocking collectives, per_device(): lax.all_to_all(grad_scaled_cols, 'seq', split_axis=0, concat_axis=1, tile...  81.1 us
    all_to_all x1, blocking collectives, per_device(): lax.all_to_all(scaled, 'seq', split_axis=1, concat_axis=0, tiled=True)  81.1 us
    unnamed x17, local copies, waits for them, and re-layouts  17.3 us
  transfers between devices with their start and end apart: 2, of which 1 were waited for; matrix products, arithmetic and copies ran while one was open for 2% of the time, Pallas kernels for 0%

commit v1 on v0

v1 whole, which is shorter than its diff:
```python
import functools

import jax
import jax.numpy as jnp
from jax import lax
from jax.experimental import pallas as pl
from jax.experimental.pallas import tpu as pltpu
from jax.sharding import PartitionSpec as P

NY, NZ, NX, NC = 2, 8, 4, 2
ROWS = 4
JL = 8
CHUNKS = 3
LANES = 128
WIDE = NC * LANES
MESH = pl.DeviceIdType.MESH
BF = jnp.bfloat16
F32 = jnp.float32


def kernel(
    acts_hbm, go_hbm, outer_hbm, inner_hbm, tw_hbm,
    gi_hbm, g_outer, g_inner, g_tw, zr, rzs,
    acts, go, o_mat, f_mat, o_t, f_t, tw_rows, tw_cols, tw_acc, inner,
    zs, pr, ps, rzr, t1, t2, gm, gia, terms, staged,
    rs_a, rs_bs, rs_b, rs_cs, rs_c, tw_send, tw_recv,
    load_sem, store_sem, z_send, z_recv, p_send, p_recv, b_send, b_recv, c_send, c_recv, t_send, t_recv,
):
    n = o_mat.shape[0]
    block = n // NZ
    seq = lax.axis_index("seq")
    dp = lax.axis_index("dp")
    y, z, x, core = seq // (NZ * NX * NC), (seq // (NX * NC)) % NZ, (seq // NC) % NX, seq % NC
    here = (y * NX + x) * NC + core
    plane = NY * NX * NC

    def seq_of(y_, z_, x_, c_):
        return ((y_ * NZ + z_) * NX + x_) * NC + c_

    def z_peer(d):
        z_ = (z + d) % NZ
        return z_, {"seq": seq_of(y, z_, x, core)}

    def plane_peer(d):
        at = (here + d) % plane
        y_, x_, c_ = at // (NX * NC), (at // NC) % NX, at % NC
        return y_, x_, c_, {"seq": seq_of(y_, z, x_, c_)}

    def remote(src, dst, send, recv, device):
        pltpu.make_async_remote_copy(
            src_ref=src, dst_ref=dst, send_sem=send, recv_sem=recv, device_id=device, device_id_type=MESH
        ).start()

    def local(src, dst, sem):
        pltpu.make_async_copy(src, dst, sem).start()

    def wait(ref, sem):
        pltpu.make_async_copy(ref, ref, sem).wait()

    def chunk_loads(k):
        lanes = pl.ds(k * WIDE, WIDE)
        return [
            pltpu.make_async_copy(acts_hbm.at[:, :, lanes], acts.at[:, :, lanes], load_sem.at[2 * k]),
            pltpu.make_async_copy(go_hbm.at[:, :, lanes], go.at[:, :, lanes], load_sem.at[2 * k + 1]),
        ]

    weight_loads = [
        pltpu.make_async_copy(inner_hbm, f_mat, load_sem.at[2 * CHUNKS]),
        pltpu.make_async_copy(tw_hbm, tw_rows, load_sem.at[2 * CHUNKS + 1]),
        pltpu.make_async_copy(outer_hbm, o_mat, load_sem.at[2 * CHUNKS + 2]),
    ]
    for k in range(CHUNKS):
        for copy in chunk_loads(k):
            copy.start()
    for copy in weight_loads:
        copy.start()

    barrier = pltpu.get_barrier_semaphore()

    @pl.loop(1, NZ)
    def _(d):
        pl.semaphore_signal(barrier, 1, device_id=z_peer(d)[1], device_id_type=MESH)

    @pl.loop(1, plane)
    def _(d):
        pl.semaphore_signal(barrier, 1, device_id=plane_peer(d)[3], device_id_type=MESH)

    for c_ in range(NC):
        pl.semaphore_signal(
            barrier, 1, device_id={"seq": seq_of(y, z, x, c_), "dp": 1 - dp}, device_id_type=MESH
        )

    def send_z(src, dst, unit):
        @pl.loop(1, NZ)
        def _(d):
            z_, device = z_peer(d)
            remote(src.at[z_], dst.at[z], z_send.at[unit], z_recv.at[unit], device)

        local(src.at[z], dst.at[z], z_recv.at[unit])

    def wait_z(dst, unit):
        wait(dst, z_recv.at[unit])

    def wait_z_sent(src, unit):
        wait(src.at[pl.ds(0, NZ - 1)], z_send.at[unit])

    def send_out(u):
        send_z(zs.at[u % CHUNKS], zr.at[u], u)

    def send_back(u):
        send_z(rzs.at[u], rzr.at[u], 2 * CHUNKS + u)

    def send_plane_out(u):
        @pl.loop(1, plane)
        def _(d):
            y_, x_, c_, device = plane_peer(d)
            remote(
                zr.at[u, :, y_ * NX + x_, c_], pr.at[u, y, :, x * NC + core], p_send.at[u], p_recv.at[u], device
            )

        local(zr.at[u, :, y * NX + x, core], pr.at[u, y, :, x * NC + core], p_recv.at[u])

    def send_plane_back(u):
        unit = 2 * CHUNKS + u
        slot = u % CHUNKS

        @pl.loop(1, plane)
        def _(d):
            y_, x_, c_, device = plane_peer(d)
            remote(
                ps.at[slot, y_, :, x_ * NC + c_], rzs.at[u, :, y * NX + x, core],
                p_send.at[unit], p_recv.at[unit], device,
            )

        local(ps.at[slot, y, :, x * NC + core], rzs.at[u, :, y * NX + x, core], p_recv.at[unit])

    def wait_plane_sent(unit):
        wait(t_blocks(), p_send.at[unit])

    def t_blocks():
        return pr.at[0].reshape(n // ROWS, ROWS * JL, LANES).at[pl.ds(0, (plane - 1) * NZ)]

    def pack(slot, value):
        @pl.loop(0, NZ)
        def _(z_):
            for h in range(NC):
                for pair in range(ROWS // 2):
                    halves = [
                        value(2 * pair + i, z_, h).reshape(block // JL, 1, JL, LANES) for i in range(2)
                    ]
                    both = jnp.concatenate(halves, axis=1).reshape(block // JL, 2 * JL, LANES)
                    zs[slot, z_, :, h, pl.ds(pair * 2 * JL, 2 * JL), :] = both.astype(BF)

    def make_gm(k):
        for copy in chunk_loads(k):
            copy.wait()

        def value(r, z_, h):
            rows, lanes = pl.ds(z_ * block, block), pl.ds(k * WIDE + h * LANES, LANES)
            return go[r, rows, lanes].astype(F32) * acts[r, rows, lanes].astype(F32)

        pack(k, value)

    def make_scaled(k):
        lanes = pl.ds(k * WIDE, WIDE)

        @pl.loop(0, ROWS)
        def _(r):
            inner[r, :, lanes] = jnp.dot(f_mat[...], acts[r, :, lanes], preferred_element_type=F32)

        def value(r, z_, h):
            rows = pl.ds(z_ * block, block)
            return inner[r, rows, pl.ds(k * WIDE + h * LANES, LANES)] * tw_cols[r, rows, :]

        pack(k, value)

    def prepare():
        for copy in weight_loads:
            copy.wait()
        f_t[...] = f_mat[...].astype(F32).T.astype(BF)
        o_t[...] = o_mat[...].astype(F32).T.astype(BF)
        for r in range(ROWS):
            tw_cols[r] = jnp.broadcast_to(tw_rows[r : r + 1, :], (LANES, n)).T
        tw_acc[...] = jnp.zeros_like(tw_acc)
        terms[...] = jnp.zeros_like(terms)

    def add_term(which, left, right):
        total = lax.dot_general(left, right, (((1,), (1,)), ((), ())), preferred_element_type=F32)
        for half in range(NC):
            part = total[:, half * (n // NC) : (half + 1) * (n // NC)]
            terms[which, half] += part.reshape(NY, NZ, NX, n // (NY * NZ * NX), n // NC)

    def mix(u):
        k, slot = u % CHUNKS, u % CHUNKS
        rows = NX * NC * ROWS * JL

        for y_ in range(NY):
            @pl.loop(0, NZ)
            def _(z_):
                at = pl.multiple_of((y_ * NZ + z_) * rows, rows)
                t1[pl.ds(at, rows), :] = pr[u, y_, z_].astype(F32).reshape(rows, LANES)

        for q in range(JL // 2):
            two = [t1[pl.ds(2 * q + i, n, stride=JL), :] for i in range(2)]
            piece = jnp.concatenate(two, axis=1).astype(BF)
            if u < CHUNKS:
                gm[k, q] = piece
                mixed = jnp.dot(o_t[...], piece, preferred_element_type=F32)
            else:
                mixed = jnp.dot(o_mat[...], piece, preferred_element_type=F32)
                add_term(0, gm[k, q], piece)
            for i in range(2):
                t2[pl.ds(2 * q + i, n, stride=JL), :] = mixed[:, i * LANES : (i + 1) * LANES]

        for y_ in range(NY):
            @pl.loop(0, NZ)
            def _(z_):
                at = pl.multiple_of((y_ * NZ + z_) * rows, rows)
                ps[slot, y_, z_] = t2[pl.ds(at, rows), :].reshape(NX * NC, ROWS * JL, LANES).astype(BF)

    def unpack(u, r, z_, h):
        tile = rzr[u, z_, :, h, pl.ds((r // 2) * 2 * JL, 2 * JL), :].astype(F32)
        return tile.reshape(block // JL, 2, JL, LANES)[:, r % 2].reshape(block, LANES)

    def finish_scaled(k):
        lanes = pl.ds(k * WIDE, WIDE)
        for r in range(ROWS):
            @pl.loop(0, NZ)
            def _(z_):
                rows = pl.ds(z_ * block, block)
                for h in range(NC):
                    gs = unpack(k, r, z_, h)
                    tw_acc[r, rows, :] += gs * inner[r, rows, pl.ds(k * WIDE + h * LANES, LANES)]
                    gia[rows, pl.ds(h * LANES, LANES)] = (gs * tw_cols[r, rows, :]).astype(BF)

            add_term(1, gia[...], acts[r, :, lanes])
            inner[r, :, lanes] = jnp.dot(f_t[...], gia[...], preferred_element_type=F32)

    def chunk_store(k):
        lanes = pl.ds(k * WIDE, WIDE)
        return pltpu.make_async_copy(staged.at[:, :, lanes], gi_hbm.at[:, :, lanes], store_sem.at[k])

    def finish_mixed(k):
        for r in range(ROWS):
            @pl.loop(0, NZ)
            def _(z_):
                rows = pl.ds(z_ * block, block)
                for h in range(NC):
                    lanes = pl.ds(k * WIDE + h * LANES, LANES)
                    gate = go[r, rows, lanes].astype(F32) * unpack(CHUNKS + k, r, z_, h)
                    staged[r, rows, lanes] = (gate + inner[r, rows, lanes]).astype(BF)

        chunk_store(k).start()

    def reduce_plane(which):
        unit = 4 * CHUNKS + which

        @pl.loop(1, plane)
        def _(d):
            y_, x_, c_, device = plane_peer(d)
            remote(
                terms.at[which, c_, y_, :, x_], rs_a.at[which, here], p_send.at[unit], p_recv.at[unit], device
            )

        local(terms.at[which, core, y, :, x], rs_a.at[which, here], p_recv.at[unit])

    def reduce_z(which):
        unit = 4 * CHUNKS + which
        wait(rs_a.at[which], p_recv.at[unit])
        total = rs_a[which, 0]
        for i in range(1, plane):
            total += rs_a[which, i]
        rs_bs[which] = total

        @pl.loop(1, NZ)
        def _(d):
            z_, device = z_peer(d)
            remote(rs_bs.at[which, z_], rs_b.at[which, z], b_send.at[which], b_recv.at[which], device)

        local(rs_bs.at[which, z], rs_b.at[which, z], b_recv.at[which])

    def reduce_last(which):
        wait(rs_b.at[which], b_recv.at[which])
        total = rs_b[which, 0]
        for i in range(1, NZ):
            total += rs_b[which, i]
        rs_cs[which] = total
        here_ = dp * NC + core

        @pl.loop(1, 2 * NC)
        def _(d):
            at = (here_ + d) % (2 * NC)
            device = {"seq": seq_of(y, z, x, at % NC), "dp": at // NC}
            remote(rs_cs.at[which], rs_c.at[which, here_], c_send.at[which], c_recv.at[which], device)

        local(rs_cs.at[which], rs_c.at[which, here_], c_recv.at[which])

    def reduced(which, out):
        wait(rs_c.at[which], c_recv.at[which])
        both = rs_c[which, :NC] + rs_c[which, NC:]
        full = jnp.concatenate([both[i] for i in range(NC)], axis=1)
        out[...] = jnp.where(core == 0, full[:ROWS], full[ROWS:])

    def send_twiddle():
        rows = [jnp.sum(tw_acc[r].T, axis=0, keepdims=True) for r in range(ROWS)]
        tw_send[...] = jnp.concatenate(rows + rows, axis=0)
        remote(tw_send, tw_recv, t_send.at[0], t_recv.at[0], {"seq": seq, "dp": 1 - dp})

    make_gm(0)
    pl.semaphore_wait(barrier, NZ - 1 + plane - 1 + NC)
    send_out(0)
    make_gm(1)
    send_out(1)
    make_gm(2)
    prepare()
    for tick in range(4 * CHUNKS):
        out = tick < 2 * CHUNKS
        if out:
            wait_z(zr.at[tick], tick)
        else:
            wait_z(rzr.at[tick - 2 * CHUNKS], tick)
        after = tick + 2
        if after < 2 * CHUNKS:
            send_out(after)
        elif after < 4 * CHUNKS:
            wait(rzs.at[after - 2 * CHUNKS], p_recv.at[after])
            send_back(after - 2 * CHUNKS)
        if out:
            send_plane_out(tick)
        if tick < CHUNKS:
            wait_z_sent(zs.at[tick % CHUNKS], tick)
            make_scaled(tick)
        if 1 <= tick <= 2 * CHUNKS:
            u = tick - 1
            wait(pr.at[u], p_recv.at[u])
            if u >= CHUNKS:
                wait_plane_sent(2 * CHUNKS + u - CHUNKS)
            mix(u)
            send_plane_back(u)
        if tick == 2 * CHUNKS:
            reduce_plane(0)
        if tick == 2 * CHUNKS + 1:
            reduce_z(0)
        if tick == 2 * CHUNKS + 2:
            reduce_last(0)
        if 2 * CHUNKS <= tick < 3 * CHUNKS:
            finish_scaled(tick - 2 * CHUNKS)
        if tick == 3 * CHUNKS - 1:
            reduce_plane(1)
            send_twiddle()
        if tick == 3 * CHUNKS:
            reduce_z(1)
            reduced(0, g_outer)
        if tick == 3 * CHUNKS + 1:
            reduce_last(1)
        if tick >= 3 * CHUNKS:
            finish_mixed(tick - 3 * CHUNKS)

    reduced(1, g_inner)
    wait(tw_recv, t_recv.at[0])
    g_tw[...] = tw_send[:ROWS] + tw_recv[:ROWS]

    for unit in range(CHUNKS, 2 * CHUNKS):
        wait_z_sent(zs.at[0], unit)
    for unit in range(2 * CHUNKS, 4 * CHUNKS):
        wait_z_sent(rzs.at[0], unit)
    for unit in range(4 * CHUNKS):
        if not 2 * CHUNKS <= unit < 3 * CHUNKS:
            wait_plane_sent(unit)
    for which in range(2):
        wait(rs_a.at[which, pl.ds(0, plane - 1)], p_send.at[4 * CHUNKS + which])
        wait(rs_b.at[which, pl.ds(0, NZ - 1)], b_send.at[which])
        wait(rs_c.at[which, pl.ds(0, 2 * NC - 1)], c_send.at[which])
    wait(tw_recv, t_send.at[0])
    for k in range(CHUNKS):
        chunk_store(k).wait()


def per_device(activations, grad_output, outer_factor, inner_factor, twiddle):
    acts, grads = activations[0], grad_output[0]
    rows, n, channels = acts.shape
    assert rows == ROWS and n == JL * NY * NZ * NX and channels == CHUNKS * WIDE
    plane, block = NY * NX * NC, ROWS * JL
    dma = pltpu.SemaphoreType.DMA
    vm = pltpu.VMEM
    units = 2 * CHUNKS
    rowed = (NZ, NY * NX, NC, block, LANES)
    columned = (NY, NZ, NX * NC, block, LANES)
    part = (n // (NY * NZ * NX), n // NC)
    small = jax.ShapeDtypeStruct((ROWS, n), F32)
    any_spec = pl.BlockSpec(memory_space=pl.ANY)
    vmem_spec = pl.BlockSpec(memory_space=pltpu.VMEM)
    slots = jax.ShapeDtypeStruct((units,) + rowed, BF)
    scratch = [
        vm((ROWS, n, channels), BF),
        vm((ROWS, n, channels), BF),
        vm((n, n), BF), vm((n, n), BF), vm((n, n), BF), vm((n, n), BF),
        vm((ROWS, n), F32),
        vm((ROWS, n, LANES), F32),
        vm((ROWS, n, LANES), F32),
        vm((ROWS, n, channels), F32),
        vm((CHUNKS,) + rowed, BF),
        vm((units,) + columned, BF),
        vm((CHUNKS,) + columned, BF),
        vm((units,) + rowed, BF),
        vm((n * JL, LANES), F32),
        vm((n * JL, LANES), F32),
        vm((CHUNKS, JL // 2, n, WIDE), BF),
        vm((n, WIDE), BF),
        vm((2, NC, NY, NZ, NX) + part, F32),
        vm((ROWS, n, channels), BF),
        vm((2, plane, NZ) + part, F32),
        vm((2, NZ) + part, F32),
        vm((2, NZ) + part, F32),
        vm((2,) + part, F32),
        vm((2, 2 * NC) + part, F32),
        vm((2 * ROWS, n), F32),
        vm((2 * ROWS, n), F32),
        dma((2 * CHUNKS + 3,)), dma((CHUNKS,)),
        dma((2 * units,)), dma((2 * units,)),
        dma((2 * units + 2,)), dma((2 * units + 2,)),
        dma((2,)), dma((2,)), dma((2,)), dma((2,)), dma((1,)), dma((1,)),
    ]
    outs = pl.pallas_call(
        kernel,
        out_shape=[jax.ShapeDtypeStruct(acts.shape, BF), small, small, small, slots, slots],
        in_specs=[any_spec] * 5,
        out_specs=[any_spec, vmem_spec, vmem_spec, vmem_spec, any_spec, any_spec],
        scratch_shapes=scratch,
        compiler_params=pltpu.CompilerParams(
            collective_id=0, has_side_effects=True, vmem_limit_bytes=60 * 2**20
        ),
        name="monarch_backward",
    )(acts, grads, outer_factor, inner_factor, twiddle)
    return outs[0][None], outs[1], outs[2], outs[3]


def solution(mesh):
    placed = (P("dp", "seq", None, None), P("dp", "seq", None, None), P(), P(), P("seq", None))
    return jax.shard_map(
        per_device,
        mesh=mesh,
        in_specs=placed,
        out_specs=(P("dp", "seq", None, None), P("seq", None), P("seq", None), P("seq", None)),
        check_vma=False,
    )
```

time: 664 us -> 298 us (0.45)
  Pallas kernels: 0 us -> 292 us
  waiting for transfers between devices: 269 us -> 0 us
  blocking collectives: 259 us -> 0 us
  local copies, waits for them, and re-layouts: 69.2 us -> 5.58 us
  matrix products: 33.1 us -> 0 us
  between operations: 14.1 us -> 0.67 us
  other arithmetic: 11 us -> 0 us
  starting transfers between devices: 6.69 us -> 0 us
    pallas_call x0 -> x1, Pallas kernels: none -> 292 us  [per_device(): pl.pallas_call(kernel, out_shape=[jax.ShapeDtypeStruct(acts.shape, BF), s...]
    psum x1 -> x0, waiting for transfers between devices: 269 us -> none  [per_device(): outer_total, inner_total = lax.psum((outer_term, inner_term), ('seq', 'dp'))]
    all_to_all x3 -> x0, blocking collectives: 253 us -> none  [the longest x1 90.7 us: per_device(): lax.all_to_all(grad_mixed, 'seq', split_axis=1, concat_axis=0, tiled=True)]
    convert_element_type x8 -> x0, local copies, waits for them, and re-layouts: 48.1 us -> none  [the longest x2 11.8 us: per_device(): grad_scaled_f = grad_scaled.astype(jnp.float32)]
    dot_general x6 -> x0, matrix products: 33.1 us -> none  [the longest x1 9.13 us: per_device(): jnp.einsum('kj,ikc->ijc', inner_factor, grad_inner_act, preferred_element...]
    unnamed x17 -> x10, local copies, waits for them, and re-layouts: 17.3 us -> 5.58 us
    convert_element_type x3 -> x0, other arithmetic: 11 us -> none  [the longest x1 5.46 us: per_device(): grad_mixed = (grads_f * acts.astype(jnp.float32)).astype(jnp.bfloat16)]
    all_to_all x1 -> x0, starting transfers between devices: 6.65 us -> none  [per_device(): lax.all_to_all(mixed_cols, 'seq', split_axis=0, concat_axis=1, tiled=True)]
  transfers between devices with their start and end apart: 2 -> 0, of which waited for: 1 -> 0; matrix products, arithmetic and copies ran while one was open for 2% -> 0% of each run, Pallas kernels for 0% -> 0%
where the time goes in v1:
time: 298 us
  Pallas kernels  292 us (98%)
  local copies, waits for them, and re-layouts  5.58 us (2%)
    pallas_call x1, Pallas kernels, per_device(): pl.pallas_call(kernel, out_shape=[jax.ShapeDtypeStruct(acts.shape, BF), s...  292 us

profile of v1, /device:TPU:1, one launch (start us, length us, event | category | flops | bytes accessed | tf_op | source)
XLA Modules:
  0.0 298.3 jit_solution(9100374033389356081)
XLA Ops:
  0.6 292.1 %monarch_backward.1 = (bf16[4,512,768]{2,1,0:T(8,128)(2,1)}, f32[4,512]{1,0:T(4,128)}, f32[4,512]{1,0:T(4,128)}, f32[4,512]{1,0:T(4,128)}, bf16[6,8,8,2,32,128]{...) custom-call(bf16[4,512,768]{2,1,0:T(8,128)(2,1)} %bitcast.3, bf16[4,512,768]{2,1,0:T(8,128)(2,1)} %bitcast.4, ...), custom_call_target="tpu_custom_call" | custom-call | tf_op jit(solution)/shard_map/monarch_backward/pallas_call | solution.py:424
  292.7 0.0 copy-start.2
  292.7 0.0 copy-start.1
  292.8 0.0 copy-start
  292.8 3.8 %copy.13 = bf16[1,4,512,768]{3,2,1,0:T(8,128)(2,1)} copy(bf16[1,4,512,768]{3,2,1,0:T(8,128)(2,1)} %bitcast.5) | data formatting | bytes 6291456
  296.5 0.0 copy-done.2
  296.5 0.6 copy.14
  297.1 0.0 copy-done.1
  297.1 0.6 copy.15
  297.7 0.0 copy-done
  297.7 0.6 copy.16
Async XLA Ops:
  292.7 3.8 %copy-start.2 = (f32[4,512]{1,0:T(4,128)S(1)}, f32[4,512]{1,0:T(4,128)}, u32[]{:S(2)}) copy-start(f32[4,512]{1,0:T(4,128)} %get-tuple-element.17) | copy-start | bytes 24580
  292.7 4.4 %copy-start.1 = (f32[4,512]{1,0:T(4,128)S(1)}, f32[4,512]{1,0:T(4,128)}, u32[]{:S(2)}) copy-start(f32[4,512]{1,0:T(4,128)} %get-tuple-element.18) | copy-start | bytes 24580
  292.8 5.0 %copy-start = (f32[4,512]{1,0:T(4,128)S(1)}, f32[4,512]{1,0:T(4,128)}, u32[]{:S(2)}) copy-start(f32[4,512]{1,0:T(4,128)} %get-tuple-element.19) | copy-start | bytes 24580

commit v2 on v1

--- a/solution.py
+++ b/solution.py
@@ -20,11 +20,11 @@
 
 def kernel(
     acts_hbm, go_hbm, outer_hbm, inner_hbm, tw_hbm,
-    gi_hbm, g_outer, g_inner, g_tw, zr, rzs,
+    gi, g_outer, g_inner, g_tw, zr, rzs,
     acts, go, o_mat, f_mat, o_t, f_t, tw_rows, tw_cols, tw_acc, inner,
-    zs, pr, ps, rzr, t1, t2, gm, gia, terms, staged,
+    zs, pr, ps, rzr, t1, t2, gm, gia, terms,
     rs_a, rs_bs, rs_b, rs_cs, rs_c, tw_send, tw_recv,
-    load_sem, store_sem, z_send, z_recv, p_send, p_recv, b_send, b_recv, c_send, c_recv, t_send, t_recv,
+    load_sem, first_sem, last_recv, z_send, z_recv, p_send, p_recv, b_send, b_recv, c_send, c_recv, t_send, t_recv,
 ):
     n = o_mat.shape[0]
     block = n // NZ
@@ -69,26 +69,48 @@
         pltpu.make_async_copy(tw_hbm, tw_rows, load_sem.at[2 * CHUNKS + 1]),
         pltpu.make_async_copy(outer_hbm, o_mat, load_sem.at[2 * CHUNKS + 2]),
     ]
-    for k in range(CHUNKS):
+
+    def nth(i):
+        return (z + NZ + (i // 2 + 1) * (1 - 2 * (i % 2))) % NZ
+
+    def first_loads(z_):
+        part = (slice(None), pl.ds(z_ * block, block), pl.ds(0, WIDE))
+        return [
+            pltpu.make_async_copy(acts_hbm.at[part], acts.at[part], first_sem.at[0, z_]),
+            pltpu.make_async_copy(go_hbm.at[part], go.at[part], first_sem.at[1, z_]),
+        ]
+
+    for i in range(2):
+        for copy in first_loads(nth(i)):
+            copy.start()
+
+    barrier = pltpu.get_barrier_semaphore()
+
+    @pl.loop(1, NZ)
+    def _(d):
+        pl.semaphore_signal(barrier, 1, device_id=z_peer(d)[1], device_id_type=MESH)
+
+    @pl.loop(1, plane)
+    def _(d):
+        pl.semaphore_signal(barrier, 1, device_id=plane_peer(d)[3], device_id_type=MESH)
+
+    for c_ in range(NC):
+        pl.semaphore_signal(
+            barrier, 1, device_id={"seq": seq_of(y, z, x, c_), "dp": 1 - dp}, device_id_type=MESH
+        )
+
+    @pl.loop(2, NZ - 1)
+    def _(i):
+        for copy in first_loads(nth(i)):
+            copy.start()
+
+    for copy in first_loads(z):
+        copy.start()
+    for k in range(1, CHUNKS):
         for copy in chunk_loads(k):
             copy.start()
     for copy in weight_loads:
         copy.start()
-
-    barrier = pltpu.get_barrier_semaphore()
-
-    @pl.loop(1, NZ)
-    def _(d):
-        pl.semaphore_signal(barrier, 1, device_id=z_peer(d)[1], device_id_type=MESH)
-
-    @pl.loop(1, plane)
-    def _(d):
-        pl.semaphore_signal(barrier, 1, device_id=plane_peer(d)[3], device_id_type=MESH)
-
-    for c_ in range(NC):
-        pl.semaphore_signal(
-            barrier, 1, device_id={"seq": seq_of(y, z, x, c_), "dp": 1 - dp}, device_id_type=MESH
-        )
 
     def send_z(src, dst, unit):
         @pl.loop(1, NZ)
@@ -109,6 +131,17 @@
 
     def send_back(u):
         send_z(rzs.at[u], rzr.at[u], 2 * CHUNKS + u)
+
+    def send_last():
+        u, unit = 2 * CHUNKS - 1, 4 * CHUNKS - 1
+
+        @pl.loop(0, NZ - 1)
+        def _(i):
+            z_ = nth(i)
+            device = {"seq": seq_of(y, z_, x, core)}
+            remote(rzs.at[u, z_], rzr.at[u, z], z_send.at[unit], last_recv.at[z], device)
+
+        local(rzs.at[u, z], rzr.at[u, z], last_recv.at[z])
 
     def send_plane_out(u):
         @pl.loop(1, plane)
@@ -140,26 +173,41 @@
     def t_blocks():
         return pr.at[0].reshape(n // ROWS, ROWS * JL, LANES).at[pl.ds(0, (plane - 1) * NZ)]
 
-    def pack(slot, value):
-        @pl.loop(0, NZ)
-        def _(z_):
-            for h in range(NC):
-                for pair in range(ROWS // 2):
-                    halves = [
-                        value(2 * pair + i, z_, h).reshape(block // JL, 1, JL, LANES) for i in range(2)
-                    ]
-                    both = jnp.concatenate(halves, axis=1).reshape(block // JL, 2 * JL, LANES)
-                    zs[slot, z_, :, h, pl.ds(pair * 2 * JL, 2 * JL), :] = both.astype(BF)
+    def pack(slot, z_, value):
+        for h in range(NC):
+            for pair in range(ROWS // 2):
+                halves = [value(2 * pair + i, z_, h).reshape(block // JL, 1, JL, LANES) for i in range(2)]
+                both = jnp.concatenate(halves, axis=1).reshape(block // JL, 2 * JL, LANES)
+                zs[slot, z_, :, h, pl.ds(pair * 2 * JL, 2 * JL), :] = both.astype(BF)
+
+    def gm_value(k):
+        def value(r, z_, h):
+            rows, lanes = pl.ds(z_ * block, block), pl.ds(k * WIDE + h * LANES, LANES)
+            return go[r, rows, lanes].astype(F32) * acts[r, rows, lanes].astype(F32)
+
+        return value
 
     def make_gm(k):
         for copy in chunk_loads(k):
             copy.wait()
 
-        def value(r, z_, h):
-            rows, lanes = pl.ds(z_ * block, block), pl.ds(k * WIDE + h * LANES, LANES)
-            return go[r, rows, lanes].astype(F32) * acts[r, rows, lanes].astype(F32)
-
-        pack(k, value)
+        @pl.loop(0, NZ)
+        def _(z_):
+            pack(k, z_, gm_value(k))
+
+    def send_first():
+        @pl.loop(0, NZ - 1)
+        def _(i):
+            z_ = nth(i)
+            for copy in first_loads(z_):
+                copy.wait()
+            pack(0, z_, gm_value(0))
+            remote(zs.at[0, z_], zr.at[0, z], z_send.at[0], z_recv.at[0], {"seq": seq_of(y, z_, x, core)})
+
+        for copy in first_loads(z):
+            copy.wait()
+        pack(0, z, gm_value(0))
+        local(zs.at[0, z], zr.at[0, z], z_recv.at[0])
 
     def make_scaled(k):
         lanes = pl.ds(k * WIDE, WIDE)
@@ -172,7 +220,9 @@
             rows = pl.ds(z_ * block, block)
             return inner[r, rows, pl.ds(k * WIDE + h * LANES, LANES)] * tw_cols[r, rows, :]
 
-        pack(k, value)
+        @pl.loop(0, NZ)
+        def _(z_):
+            pack(k, z_, value)
 
     def prepare():
         for copy in weight_loads:
@@ -236,21 +286,27 @@
             add_term(1, gia[...], acts[r, :, lanes])
             inner[r, :, lanes] = jnp.dot(f_t[...], gia[...], preferred_element_type=F32)
 
-    def chunk_store(k):
-        lanes = pl.ds(k * WIDE, WIDE)
-        return pltpu.make_async_copy(staged.at[:, :, lanes], gi_hbm.at[:, :, lanes], store_sem.at[k])
+    def finish_block(k, z_):
+        rows = pl.ds(z_ * block, block)
+        for r in range(ROWS):
+            for h in range(NC):
+                lanes = pl.ds(k * WIDE + h * LANES, LANES)
+                gate = go[r, rows, lanes].astype(F32) * unpack(CHUNKS + k, r, z_, h)
+                gi[r, rows, lanes] = (gate + inner[r, rows, lanes]).astype(BF)
 
     def finish_mixed(k):
-        for r in range(ROWS):
-            @pl.loop(0, NZ)
-            def _(z_):
-                rows = pl.ds(z_ * block, block)
-                for h in range(NC):
-                    lanes = pl.ds(k * WIDE + h * LANES, LANES)
-                    gate = go[r, rows, lanes].astype(F32) * unpack(CHUNKS + k, r, z_, h)
-                    staged[r, rows, lanes] = (gate + inner[r, rows, lanes]).astype(BF)
-
-        chunk_store(k).start()
+        @pl.loop(0, NZ)
+        def _(z_):
+            finish_block(k, z_)
+
+    def finish_last():
+        k = CHUNKS - 1
+
+        @pl.loop(0, NZ)
+        def _(i):
+            z_ = jnp.where(i == 0, z, nth(jnp.maximum(i - 1, 0)))
+            wait(rzr.at[2 * CHUNKS - 1, z_], last_recv.at[z_])
+            finish_block(k, z_)
 
     def reduce_plane(which):
         unit = 4 * CHUNKS + which
@@ -306,9 +362,22 @@
         tw_send[...] = jnp.concatenate(rows + rows, axis=0)
         remote(tw_send, tw_recv, t_send.at[0], t_recv.at[0], {"seq": seq, "dp": 1 - dp})
 
-    make_gm(0)
+    def drain():
+        for unit in range(CHUNKS, 2 * CHUNKS):
+            wait_z_sent(zs.at[0], unit)
+        for unit in range(2 * CHUNKS, 4 * CHUNKS - 1):
+            wait_z_sent(rzs.at[0], unit)
+        for unit in range(4 * CHUNKS):
+            if not 2 * CHUNKS <= unit < 3 * CHUNKS:
+                wait_plane_sent(unit)
+        for which in range(2):
+            wait(rs_a.at[which, pl.ds(0, plane - 1)], p_send.at[4 * CHUNKS + which])
+            wait(rs_b.at[which, pl.ds(0, NZ - 1)], b_send.at[which])
+            wait(rs_c.at[which, pl.ds(0, 2 * NC - 1)], c_send.at[which])
+        wait(tw_recv, t_send.at[0])
+
     pl.semaphore_wait(barrier, NZ - 1 + plane - 1 + NC)
-    send_out(0)
+    send_first()
     make_gm(1)
     send_out(1)
     make_gm(2)
@@ -317,14 +386,21 @@
         out = tick < 2 * CHUNKS
         if out:
             wait_z(zr.at[tick], tick)
-        else:
+        elif tick < 4 * CHUNKS - 1:
             wait_z(rzr.at[tick - 2 * CHUNKS], tick)
+        if tick == 2 * CHUNKS + 1:
+            reduce_z(0)
+        if tick == 3 * CHUNKS:
+            reduce_z(1)
         after = tick + 2
         if after < 2 * CHUNKS:
             send_out(after)
         elif after < 4 * CHUNKS:
             wait(rzs.at[after - 2 * CHUNKS], p_recv.at[after])
-            send_back(after - 2 * CHUNKS)
+            if after < 4 * CHUNKS - 1:
+                send_back(after - 2 * CHUNKS)
+            else:
+                send_last()
         if out:
             send_plane_out(tick)
         if tick < CHUNKS:
@@ -339,8 +415,6 @@
             send_plane_back(u)
         if tick == 2 * CHUNKS:
             reduce_plane(0)
-        if tick == 2 * CHUNKS + 1:
-            reduce_z(0)
         if tick == 2 * CHUNKS + 2:
             reduce_last(0)
         if 2 * CHUNKS <= tick < 3 * CHUNKS:
@@ -349,31 +423,30 @@
             reduce_plane(1)
             send_twiddle()
         if tick == 3 * CHUNKS:
-            reduce_z(1)
             reduced(0, g_outer)
         if tick == 3 * CHUNKS + 1:
             reduce_last(1)
-        if tick >= 3 * CHUNKS:
+        if 3 * CHUNKS <= tick < 4 * CHUNKS - 1:
             finish_mixed(tick - 3 * CHUNKS)
 
     reduced(1, g_inner)
     wait(tw_recv, t_recv.at[0])
     g_tw[...] = tw_send[:ROWS] + tw_recv[:ROWS]
 
-    for unit in range(CHUNKS, 2 * CHUNKS):
-        wait_z_sent(zs.at[0], unit)
-    for unit in range(2 * CHUNKS, 4 * CHUNKS):
-        wait_z_sent(rzs.at[0], unit)
-    for unit in range(4 * CHUNKS):
-        if not 2 * CHUNKS <= unit < 3 * CHUNKS:
-            wait_plane_sent(unit)
-    for which in range(2):
-        wait(rs_a.at[which, pl.ds(0, plane - 1)], p_send.at[4 * CHUNKS + which])
-        wait(rs_b.at[which, pl.ds(0, NZ - 1)], b_send.at[which])
-        wait(rs_c.at[which, pl.ds(0, 2 * NC - 1)], c_send.at[which])
-    wait(tw_recv, t_send.at[0])
-    for k in range(CHUNKS):
-        chunk_store(k).wait()
+    drain()
+    finish_last()
+    wait_z_sent(rzs.at[0], 4 * CHUNKS - 1)
+
+
+def hand_over(*refs):
+    sems = refs[-1]
+    pairs = [(refs[0].at[r], refs[4].at[r]) for r in range(ROWS)]
+    pairs += list(zip(refs[1:4], refs[5:8]))
+    copies = [pltpu.make_async_copy(src, dst, sems.at[i]) for i, (src, dst) in enumerate(pairs)]
+    for copy in copies:
+        copy.start()
+    for copy in copies:
+        copy.wait()
 
 
 def per_device(activations, grad_output, outer_factor, inner_factor, twiddle):
@@ -408,7 +481,6 @@
         vm((CHUNKS, JL // 2, n, WIDE), BF),
         vm((n, WIDE), BF),
         vm((2, NC, NY, NZ, NX) + part, F32),
-        vm((ROWS, n, channels), BF),
         vm((2, plane, NZ) + part, F32),
         vm((2, NZ) + part, F32),
         vm((2, NZ) + part, F32),
@@ -416,22 +488,31 @@
         vm((2, 2 * NC) + part, F32),
         vm((2 * ROWS, n), F32),
         vm((2 * ROWS, n), F32),
-        dma((2 * CHUNKS + 3,)), dma((CHUNKS,)),
+        dma((2 * CHUNKS + 3,)), dma((2, NZ)), dma((NZ,)),
         dma((2 * units,)), dma((2 * units,)),
         dma((2 * units + 2,)), dma((2 * units + 2,)),
         dma((2,)), dma((2,)), dma((2,)), dma((2,)), dma((1,)), dma((1,)),
     ]
     outs = pl.pallas_call(
         kernel,
-        out_shape=[jax.ShapeDtypeStruct(acts.shape, BF), small, small, small, slots, slots],
+        out_shape=[pltpu.VMEM(acts.shape, BF)] + [pltpu.VMEM(small.shape, F32)] * 3 + [slots, slots],
         in_specs=[any_spec] * 5,
-        out_specs=[any_spec, vmem_spec, vmem_spec, vmem_spec, any_spec, any_spec],
+        out_specs=[vmem_spec, vmem_spec, vmem_spec, vmem_spec, any_spec, any_spec],
         scratch_shapes=scratch,
         compiler_params=pltpu.CompilerParams(
-            collective_id=0, has_side_effects=True, vmem_limit_bytes=60 * 2**20
+            collective_id=0, has_side_effects=True, vmem_limit_bytes=52 * 2**20
         ),
         name="monarch_backward",
     )(acts, grads, outer_factor, inner_factor, twiddle)
+    outs = pl.pallas_call(
+        hand_over,
+        out_shape=[jax.ShapeDtypeStruct(o.shape, o.dtype) for o in outs[:4]],
+        in_specs=[any_spec] * 4,
+        out_specs=[any_spec] * 4,
+        scratch_shapes=[dma((ROWS + 3,))],
+        compiler_params=pltpu.CompilerParams(vmem_limit_bytes=4 * 2**20),
+        name="hand_over",
+    )(*outs[:4])
     return outs[0][None], outs[1], outs[2], outs[3]
 
 

time: 298 us -> 288 us (0.966)
  local copies, waits for them, and re-layouts: 5.58 us -> 0 us
  Pallas kernels: 292 us -> 287 us
    unnamed x10 -> x0, local copies, waits for them, and re-layouts: 5.58 us -> none
    pallas_call x1 -> x2, Pallas kernels: 292 us -> 287 us  [the longest x1 285 us: per_device(): pl.pallas_call(kernel, out_shape=[pltpu.VMEM(acts.shape, BF)] + [pltpu.VM...]
where the time goes in v2:
time: 288 us
  Pallas kernels  287 us (100%)
    pallas_call x1, Pallas kernels, per_device(): pl.pallas_call(kernel, out_shape=[pltpu.VMEM(acts.shape, BF)] + [pltpu.VM...  285 us

profile of v2, /device:TPU:1, one launch (start us, length us, event | category | flops | bytes accessed | tf_op | source)
XLA Modules:
  0.0 287.8 jit_solution(16425143170746802448)
XLA Ops:
  0.6 285.4 %monarch_backward.1 = (bf16[4,512,768]{2,1,0:T(8,128)(2,1)S(1)}, f32[4,512]{1,0:T(4,128)S(1)}, f32[4,512]{1,0:T(4,128)S(1)}, f32[4,512]{1,0:T(4,128)S(1)}, bf16[...) custom-call(bf16[4,512,768]{2,1,0:T(8,128)(2,1)} %bitcast.3, bf16[4,512,768]{2,1,0:T(8,128)(2,1)} %bitcast.4, ...), custom_call_target="tpu_custom_call" | custom-call | tf_op jit(solution)/shard_map/monarch_backward/pallas_call | solution.py:496
  286.1 1.7 hand_over.1

commit v3 on v2

--- a/solution.py
+++ b/solution.py
@@ -9,6 +9,8 @@
 
 NY, NZ, NX, NC = 2, 8, 4, 2
 ROWS = 4
+NDP = 2
+QUARTERS = NDP * NC
 JL = 8
 CHUNKS = 3
 LANES = 128
@@ -30,20 +32,23 @@
     block = n // NZ
     seq = lax.axis_index("seq")
     dp = lax.axis_index("dp")
-    y, z, x, core = seq // (NZ * NX * NC), (seq // (NX * NC)) % NZ, (seq // NC) % NX, seq % NC
+    div, rem = lax.div, lax.rem
+    y, z, x, core = div(seq, NZ * NX * NC), rem(div(seq, NX * NC), NZ), rem(div(seq, NC), NX), rem(seq, NC)
     here = (y * NX + x) * NC + core
     plane = NY * NX * NC
 
     def seq_of(y_, z_, x_, c_):
         return ((y_ * NZ + z_) * NX + x_) * NC + c_
 
+    def in_plane(at):
+        return div(at, NX * NC), rem(div(at, NC), NX), rem(at, NC)
+
     def z_peer(d):
-        z_ = (z + d) % NZ
+        z_ = rem(z + d, NZ)
         return z_, {"seq": seq_of(y, z_, x, core)}
 
     def plane_peer(d):
-        at = (here + d) % plane
-        y_, x_, c_ = at // (NX * NC), (at // NC) % NX, at % NC
+        y_, x_, c_ = in_plane(rem(here + d, plane))
         return y_, x_, c_, {"seq": seq_of(y_, z, x_, c_)}
 
     def remote(src, dst, send, recv, device):
@@ -71,7 +76,7 @@
     ]
 
     def nth(i):
-        return (z + NZ + (i // 2 + 1) * (1 - 2 * (i % 2))) % NZ
+        return rem(z + NZ + (i // 2 + 1) * (1 - 2 * (i % 2)), NZ)
 
     def first_loads(z_):
         part = (slice(None), pl.ds(z_ * block, block), pl.ds(0, WIDE))
@@ -86,18 +91,17 @@
 
     barrier = pltpu.get_barrier_semaphore()
 
-    @pl.loop(1, NZ)
-    def _(d):
-        pl.semaphore_signal(barrier, 1, device_id=z_peer(d)[1], device_id_type=MESH)
-
-    @pl.loop(1, plane)
-    def _(d):
-        pl.semaphore_signal(barrier, 1, device_id=plane_peer(d)[3], device_id_type=MESH)
-
-    for c_ in range(NC):
-        pl.semaphore_signal(
-            barrier, 1, device_id={"seq": seq_of(y, z, x, c_), "dp": 1 - dp}, device_id_type=MESH
-        )
+    def greet(device):
+        pl.semaphore_signal(barrier, 1, device_id=device, device_id_type=MESH)
+
+    for d in range(1, NZ):
+        greet(z_peer(d)[1])
+    for d in range(plane):
+        dy, dx, dc = d // (NX * NC), d // NC % NX, d % NC
+        near = seq_of(1 - y if dy else y, z, rem(x + dx, NX), 1 - core if dc else core)
+        if d:
+            greet({"seq": near})
+        greet({"seq": near, "dp": 1 - dp})
 
     @pl.loop(2, NZ - 1)
     def _(i):
@@ -112,10 +116,16 @@
     for copy in weight_loads:
         copy.start()
 
+    def ascending(i):
+        return i + jnp.where(i >= z, 1, 0)
+
     def send_z(src, dst, unit):
-        @pl.loop(1, NZ)
-        def _(d):
-            z_, device = z_peer(d)
+        late = unit >= 4 * CHUNKS - 3
+
+        @pl.loop(0, NZ - 1)
+        def _(i):
+            z_ = ascending(i) if late else rem(z + 1 + i, NZ)
+            device = {"seq": seq_of(y, z_, x, core)}
             remote(src.at[z_], dst.at[z], z_send.at[unit], z_recv.at[unit], device)
 
         local(src.at[z], dst.at[z], z_recv.at[unit])
@@ -137,7 +147,7 @@
 
         @pl.loop(0, NZ - 1)
         def _(i):
-            z_ = nth(i)
+            z_ = ascending(i)
             device = {"seq": seq_of(y, z_, x, core)}
             remote(rzs.at[u, z_], rzr.at[u, z], z_send.at[unit], last_recv.at[z], device)
 
@@ -236,9 +246,10 @@
 
     def add_term(which, left, right):
         total = lax.dot_general(left, right, (((1,), (1,)), ((), ())), preferred_element_type=F32)
-        for half in range(NC):
-            part = total[:, half * (n // NC) : (half + 1) * (n // NC)]
-            terms[which, half] += part.reshape(NY, NZ, NX, n // (NY * NZ * NX), n // NC)
+        lanes = n // QUARTERS
+        for q in range(QUARTERS):
+            part = total[:, q * lanes : (q + 1) * lanes]
+            terms[which, q] += part.reshape(NY, NZ, NX, n // (NY * NZ * NX), lanes)
 
     def mix(u):
         k, slot = u % CHUNKS, u % CHUNKS
@@ -310,21 +321,25 @@
 
     def reduce_plane(which):
         unit = 4 * CHUNKS + which
-
-        @pl.loop(1, plane)
+        own = dp * plane + here
+
+        @pl.loop(1, NDP * plane)
         def _(d):
-            y_, x_, c_, device = plane_peer(d)
+            at = rem(own + d, NDP * plane)
+            dp_ = div(at, plane)
+            y_, x_, c_ = in_plane(rem(at, plane))
+            device = {"seq": seq_of(y_, z, x_, c_), "dp": dp_}
             remote(
-                terms.at[which, c_, y_, :, x_], rs_a.at[which, here], p_send.at[unit], p_recv.at[unit], device
+                terms.at[which, dp_ * NC + c_, y_, :, x_], rs_a.at[which, own], p_send.at[unit], p_recv.at[unit], device
             )
 
-        local(terms.at[which, core, y, :, x], rs_a.at[which, here], p_recv.at[unit])
+        local(terms.at[which, dp * NC + core, y, :, x], rs_a.at[which, own], p_recv.at[unit])
 
     def reduce_z(which):
         unit = 4 * CHUNKS + which
         wait(rs_a.at[which], p_recv.at[unit])
         total = rs_a[which, 0]
-        for i in range(1, plane):
+        for i in range(1, NDP * plane):
             total += rs_a[which, i]
         rs_bs[which] = total
 
@@ -343,18 +358,17 @@
         rs_cs[which] = total
         here_ = dp * NC + core
 
-        @pl.loop(1, 2 * NC)
+        @pl.loop(1, QUARTERS)
         def _(d):
-            at = (here_ + d) % (2 * NC)
-            device = {"seq": seq_of(y, z, x, at % NC), "dp": at // NC}
+            at = rem(here_ + d, QUARTERS)
+            device = {"seq": seq_of(y, z, x, rem(at, NC)), "dp": div(at, NC)}
             remote(rs_cs.at[which], rs_c.at[which, here_], c_send.at[which], c_recv.at[which], device)
 
         local(rs_cs.at[which], rs_c.at[which, here_], c_recv.at[which])
 
     def reduced(which, out):
         wait(rs_c.at[which], c_recv.at[which])
-        both = rs_c[which, :NC] + rs_c[which, NC:]
-        full = jnp.concatenate([both[i] for i in range(NC)], axis=1)
+        full = jnp.concatenate([rs_c[which, q] for q in range(QUARTERS)], axis=1)
         out[...] = jnp.where(core == 0, full[:ROWS], full[ROWS:])
 
     def send_twiddle():
@@ -371,12 +385,12 @@
             if not 2 * CHUNKS <= unit < 3 * CHUNKS:
                 wait_plane_sent(unit)
         for which in range(2):
-            wait(rs_a.at[which, pl.ds(0, plane - 1)], p_send.at[4 * CHUNKS + which])
+            wait(rs_a.at[which, pl.ds(0, NDP * plane - 1)], p_send.at[4 * CHUNKS + which])
             wait(rs_b.at[which, pl.ds(0, NZ - 1)], b_send.at[which])
-            wait(rs_c.at[which, pl.ds(0, 2 * NC - 1)], c_send.at[which])
+            wait(rs_c.at[which, pl.ds(0, QUARTERS - 1)], c_send.at[which])
         wait(tw_recv, t_send.at[0])
 
-    pl.semaphore_wait(barrier, NZ - 1 + plane - 1 + NC)
+    pl.semaphore_wait(barrier, NZ - 1 + plane - 1 + plane)
     send_first()
     make_gm(1)
     send_out(1)
@@ -459,7 +473,7 @@
     units = 2 * CHUNKS
     rowed = (NZ, NY * NX, NC, block, LANES)
     columned = (NY, NZ, NX * NC, block, LANES)
-    part = (n // (NY * NZ * NX), n // NC)
+    part = (n // (NY * NZ * NX), n // QUARTERS)
     small = jax.ShapeDtypeStruct((ROWS, n), F32)
     any_spec = pl.BlockSpec(memory_space=pl.ANY)
     vmem_spec = pl.BlockSpec(memory_space=pltpu.VMEM)
@@ -480,12 +494,12 @@
         vm((n * JL, LANES), F32),
         vm((CHUNKS, JL // 2, n, WIDE), BF),
         vm((n, WIDE), BF),
-        vm((2, NC, NY, NZ, NX) + part, F32),
-        vm((2, plane, NZ) + part, F32),
+        vm((2, QUARTERS, NY, NZ, NX) + part, F32),
+        vm((2, NDP * plane, NZ) + part, F32),
         vm((2, NZ) + part, F32),
         vm((2, NZ) + part, F32),
         vm((2,) + part, F32),
-        vm((2, 2 * NC) + part, F32),
+        vm((2, QUARTERS) + part, F32),
         vm((2 * ROWS, n), F32),
         vm((2 * ROWS, n), F32),
         dma((2 * CHUNKS + 3,)), dma((2, NZ)), dma((NZ,)),

time: 288 us -> 286 us (level); the launches traced: 288 us -> 282 us
  Pallas kernels: 287 us -> 282 us
    pallas_call x1, Pallas kernels: 285 us -> 280 us  [per_device(): pl.pallas_call(kernel, out_shape=[pltpu.VMEM(acts.shape, BF)] + [pltpu.VM...]
where the time goes in v3:
time: 286 us; the launch traced here: 282 us
  Pallas kernels  282 us (99%)
    pallas_call x1, Pallas kernels, per_device(): pl.pallas_call(kernel, out_shape=[pltpu.VMEM(acts.shape, BF)] + [pltpu.VM...  280 us

profile of v3, /device:TPU:1, one launch (start us, length us, event | category | flops | bytes accessed | tf_op | source)
XLA Modules:
  0.0 282.3 jit_solution(8464570387982772712)
XLA Ops:
  0.6 280.0 %monarch_backward.1 = (bf16[4,512,768]{2,1,0:T(8,128)(2,1)S(1)}, f32[4,512]{1,0:T(4,128)S(1)}, f32[4,512]{1,0:T(4,128)S(1)}, f32[4,512]{1,0:T(4,128)S(1)}, bf16[...) custom-call(bf16[4,512,768]{2,1,0:T(8,128)(2,1)} %bitcast.3, bf16[4,512,768]{2,1,0:T(8,128)(2,1)} %bitcast.4, ...), custom_call_target="tpu_custom_call" | custom-call | tf_op jit(solution)/shard_map/monarch_backward/pallas_call | solution.py:510
  280.6 1.7 hand_over.1

commit v4 on v3

--- a/solution.py
+++ b/solution.py
@@ -205,13 +205,21 @@
         def _(z_):
             pack(k, z_, gm_value(k))
 
+    def make_first(i):
+        z_ = nth(i)
+        for copy in first_loads(z_):
+            copy.wait()
+        pack(0, z_, gm_value(0))
+
     def send_first():
         @pl.loop(0, NZ - 1)
         def _(i):
             z_ = nth(i)
-            for copy in first_loads(z_):
-                copy.wait()
-            pack(0, z_, gm_value(0))
+
+            @pl.when(i >= 2)
+            def _():
+                make_first(i)
+
             remote(zs.at[0, z_], zr.at[0, z], z_send.at[0], z_recv.at[0], {"seq": seq_of(y, z_, x, core)})
 
         for copy in first_loads(z):
@@ -389,6 +397,10 @@
             wait(rs_b.at[which, pl.ds(0, NZ - 1)], b_send.at[which])
             wait(rs_c.at[which, pl.ds(0, QUARTERS - 1)], c_send.at[which])
         wait(tw_recv, t_send.at[0])
+
+    @pl.loop(0, 2)
+    def _(i):
+        make_first(i)
 
     pl.semaphore_wait(barrier, NZ - 1 + plane - 1 + plane)
     send_first()

time: 286 us -> 286 us (level)
  no operation moved by 1% of the time
where the time goes in v4:
time: 286 us; the launch traced here: 282 us
  Pallas kernels  282 us (99%)
    pallas_call x1, Pallas kernels, per_device(): pl.pallas_call(kernel, out_shape=[pltpu.VMEM(acts.shape, BF)] + [pltpu.VM...  280 us

profile of v4, /device:TPU:1, one launch (start us, length us, event | category | flops | bytes accessed | tf_op | source)
XLA Modules:
  0.0 282.3 jit_solution(12231379815347348104)
XLA Ops:
  0.6 279.9 %monarch_backward.1 = (bf16[4,512,768]{2,1,0:T(8,128)(2,1)S(1)}, f32[4,512]{1,0:T(4,128)S(1)}, f32[4,512]{1,0:T(4,128)S(1)}, f32[4,512]{1,0:T(4,128)S(1)}, bf16[...) custom-call(bf16[4,512,768]{2,1,0:T(8,128)(2,1)} %bitcast.3, bf16[4,512,768]{2,1,0:T(8,128)(2,1)} %bitcast.4, ...), custom_call_target="tpu_custom_call" | custom-call | tf_op jit(solution)/shard_map/monarch_backward/pallas_call | solution.py:522
  280.6 1.7 hand_over.1
